TPU v7x, 32 devices: a whole 2x2x4 slice. The times are simulated.
32 devices in a mesh: tile: 8 (over y, x, core), batch: 4 (over z).
Axes of the slice: x: 2, y: 2, z: 4, core: 2. Of those that a mesh axis runs over, the one named last changes fastest.
Arguments:
- object_tiles: float32 [8, 2, 384, 384], P('tile'), may hold values from -5 to 5
- probe: bfloat16 [8, 2, 256, 256], replicated, may hold values from -4 to 4
- offsets: int32 [8, 4, 2], P('tile', 'batch'), may hold values from 0 to 383, as said below
- amplitude: float32 [8, 4, 256, 256], P('tile', 'batch'), may hold values from 0.3 to 3
Outputs:
- object_grad: float32 [8, 2, 384, 384], P('tile')
- probe_grad: float32 [8, 2, 256, 256], replicated
Inputs may be any that keep to these rules, and one draw needn't show every extreme that they name: `offsets`: offsets are such that every patch lies inside the region: in tiles of the last tile row the row offset is at most 128, in tiles of the last tile column the column offset likewise.
All inputs are finite; a program needn't handle non-finite values.
Results may differ from a plain program's by a relative error of at most 0.0003.
Values sent between devices are 32-bit elements; how exact they have to be, the bound alone decides.
A program may use at most 64 MiB of HBM per device.

v0:
```python
import math

import jax
import jax.numpy as jnp
from jax import lax
from jax.sharding import PartitionSpec as P

TILE_COLS = 4


def passed_along(block, axis, distance):
    devices = range(lax.axis_size(axis))
    route = [(i - distance, i) for i in devices if i - distance in devices]
    return lax.ppermute(block, axis, route)


def dft_blocks(pattern):
    counter = jnp.arange(pattern, dtype=jnp.int32)
    phase_index = counter[:, None] * counter[None, :] % pattern
    angles = phase_index.astype(jnp.float32) * (2.0 * math.pi / pattern)
    cosine = jnp.cos(angles) / math.sqrt(pattern)
    sine_table = jnp.sin(angles) / math.sqrt(pattern)
    first_table = jnp.stack(
        [jnp.stack([cosine, sine_table], axis=1), jnp.stack([-sine_table, cosine], axis=1)], axis=0
    )
    second_table = jnp.stack(
        [jnp.stack([cosine, -sine_table], axis=1), jnp.stack([sine_table, cosine], axis=1)], axis=0
    )
    return (first_table, second_table)


def transform(wave, left_table, right_table):
    half_done = jnp.einsum("ajbk,mbkc->majc", left_table, wave, precision=lax.Precision.HIGHEST)
    return jnp.einsum("mbjk,bkac->majc", half_done, right_table, precision=lax.Precision.HIGHEST)


def return_margins(grad_ext, tile_side, pattern):
    lower_part = passed_along(grad_ext[:, tile_side:, :], "tile", TILE_COLS)
    upper_part = grad_ext[:, :tile_side, :].at[:, :pattern, :].add(lower_part)
    right_part = passed_along(upper_part[:, :, tile_side:], "tile", 1)
    return upper_part[:, :, :tile_side].at[:, :, :pattern].add(right_part)


def shards(object_tiles, probe, offsets, amplitude):
    own_tile = object_tiles[0]
    pattern = probe.shape[-1]
    tile_side = own_tile.shape[-1]
    right_strip = passed_along(own_tile[:, :, :pattern], "tile", -1)
    widened = jnp.concatenate([own_tile, right_strip], axis=2)
    lower_strip = passed_along(widened[:, :pattern, :], "tile", -TILE_COLS)
    extended = jnp.concatenate([widened, lower_strip], axis=1)
    first_table, second_table = dft_blocks(pattern)
    probe_wide = probe.astype(jnp.float32)
    probe_re = probe_wide[:, 0]
    probe_im = probe_wide[:, 1]
    grad_ext = jnp.zeros_like(extended)
    zero_index = jnp.int32(0)
    row_at = offsets[0, 0, 0]
    col_at = offsets[0, 0, 1]
    object_patch = lax.dynamic_slice(extended, (zero_index, row_at, col_at), (2, pattern, pattern))
    exit_wave = jnp.stack(
        [
            probe_re * object_patch[0] - probe_im * object_patch[1],
            probe_re * object_patch[1] + probe_im * object_patch[0],
        ],
        axis=1,
    )
    far_field = transform(exit_wave, first_table, second_table)
    intensity = jnp.sum(far_field * far_field, axis=(0, 1))
    factor = 1.0 - amplitude[0, 0] / jnp.sqrt(intensity + 0.01)
    back_wave = transform(far_field * factor, second_table, first_table)
    back_re = back_wave[:, 0]
    back_im = back_wave[:, 1]
    object_term = jnp.stack(
        [
            jnp.sum(probe_re * back_re + probe_im * back_im, axis=0),
            jnp.sum(probe_re * back_im - probe_im * back_re, axis=0),
        ]
    )
    grad_ext = lax.dynamic_update_slice(grad_ext, object_term, (zero_index, row_at, col_at))
    grad_probe = jnp.stack(
        [
            object_patch[0] * back_re + object_patch[1] * back_im,
            object_patch[0] * back_im - object_patch[1] * back_re,
        ],
        axis=1,
    )
    object_grad = lax.psum(return_margins(grad_ext, tile_side, pattern), "batch")
    positions = lax.axis_size("tile") * lax.axis_size("batch") * offsets.shape[1]
    summed = lax.psum(grad_probe, ("tile", "batch"))
    return (object_grad[None], summed / math.sqrt(positions))


def solution(mesh):
    placed = (
        P("tile", None, None, None),
        P(),
        P("tile", "batch", None),
        P("tile", "batch", None, None),
    )
    return jax.shard_map(
        shards,
        mesh=mesh,
        in_specs=placed,
        out_specs=(P("tile", None, None, None), P()),
        check_vma=False,
    )
```

profile of v0, /device:TPU:0, one launch (start us, length us, event | category | flops | bytes accessed | tf_op | source)
XLA Modules:
  0.0 334.3 jit_solution(6784778717710042715)
XLA Ops:
  7.2 0.0 all-reduce.5.cloned.1.call-start
  7.2 1.3 slice.115
  8.5 1.3 collective-permute-start
  9.8 2.9 collective-permute-done
  12.7 0.9 copy-done.4
  13.6 1.2 pad_maximum_fusion.1
  14.7 1.3 collective-permute-start.1
  16.0 0.6 fusion.36
  19.1 2.9 copy.13
  22.0 2.5 convert_element_type.35
  24.5 1.1 copy.17
  26.8 1.0 fusion.34
  27.8 1.1 sine_multiply_fusion
  28.9 0.2 fusion.23
  29.1 26.9 %collective-permute-done.1 = f32[2,256,640]{2,1,0:T(8,128)} collective-permute-done((f32[2,256,640]{2,1,0:T(8,128)}, f32[2,256,640]{2,1,0:T(8,128)}, u32[]{:S(2)}, u32[]{:S(2)}) %collective-permute-start.1) | collective-permute-done | bytes 1310752 | tf_op jit(solution)/shard_map/ppermute | solution.py:14
  55.9 1.7 fusion.25
  57.6 0.1 copy.15
  57.8 0.1 copy.16
  57.9 2.8 multiply_subtract_fusion.1
  60.7 6.9 %fusion.8 = f32[8,256,2,256,1]{1,3,4,2,0:T(8,128)S(1)} fusion(f32[1,256,2,256]{1,3,2,0:T(8,128)S(1)} %get-tuple-element.39, f32[1,256,2,256]{1,3,2,0:T(8,128)S(1)} %get-tuple-element.44, f32[8,1,256,256]{2,3,0,1:T(8,128)S(1)} %get-tuple-element.35, f32[8,1,256,256]{2,3,0,1:T(8,128)S(1)} %get-tuple-element.34), kind=kOutput, calls=%fused_computation.12 | convolution fusion | flops 6443761664 | bytes 9437184 | tf_op jit(solution)/shard_map/ajbk,mbkc->majc/dot_general | solution.py:33
  67.6 7.6 %fusion.4 = (f32[256,256]{0,1:T(8,128)S(1)}, f32[2,256,8,256,1]{3,1,4,2,0:T(8,128)S(1)}) fusion(f32[8,256,2,256,1]{1,3,4,2,0:T(8,128)S(1)} %fusion.8, f32[1,256,2,256]{1,3,0,2:T(8,128)S(1)} %get-tuple-element.45, f32[1,256,2,256]{1,3,0,2:T(8,128)S(1)} %get-tuple-element.38), kind=kOutput, calls=%fused_computation.8 | convolution fusion | flops 6444744704 | bytes 9699328 | tf_op jit(solution)/shard_map/mbjk,bkac->majc/dot_general | solution.py:34
  75.3 17.2 %fusion.6 = f32[8,256,2,256,1]{1,3,4,2,0:T(8,128)S(1)} fusion(f32[2,256,8,256,1]{3,1,4,2,0:T(8,128)S(1)} %get-tuple-element.49, f32[256,256]{0,1:T(8,128)S(1)} %fusion.30, f32[1,256,2,256]{1,3,0,2:T(8,128)S(1)} %get-tuple-element.45, f32[1,256,2,256]{1,3,0,2:T(8,128)S(1)} %get-tuple-element.38), kind=kOutput, calls=%fused_computation.10 | convolution fusion | flops 6443761664 | bytes 9699328 | tf_op jit(solution)/shard_map/ajbk,mbkc->majc/dot_general | solution.py:33
  92.5 0.0 copy-start
  92.5 7.2 %fusion.10 = f32[8,2,256,256]{2,3,0,1:T(8,128)S(1)} fusion(f32[8,256,2,256,1]{1,3,4,2,0:T(8,128)S(1)} %fusion.6, f32[1,256,2,256]{1,3,2,0:T(8,128)S(1)} %get-tuple-element.39, f32[1,256,2,256]{1,3,2,0:T(8,128)S(1)} %get-tuple-element.44), kind=kOutput, calls=%fused_computation.17 | convolution fusion | flops 6442713088 | bytes 9437184 | tf_op jit(solution)/shard_map/mbjk,bkac->majc/dot_general | solution.py:34
  99.7 3.1 multiply_add_fusion
  102.8 1.0 copy.19
  103.8 0.2 broadcast_in_dim.4
  104.0 7.0 %dynamic_update_slice.3 = f32[2,640,640]{2,1,0:T(8,128)S(1)} dynamic-update-slice(f32[2,640,640]{2,1,0:T(8,128)S(1)} %broadcast_in_dim.4, f32[2,256,256]{2,1,0:T(8,128)} %copy.19, s32[]{:T(128)} %constant.76.clone.1, s32[]{:T(128)S(6)} %select_n.45, s32[]{:T(128)S(6)} %select_n.46) | dynamic-update-slice | bytes 1048580 | tf_op jit(solution)/shard_map/dynamic_update_slice | solution.py:80
  111.0 1.2 slice.123
  112.2 4.4 %collective-permute-start.2 = (f32[2,256,640]{2,1,0:T(8,128)}, f32[2,256,640]{2,1,0:T(8,128)}, u32[]{:S(2)}, u32[]{:S(2)}) collective-permute-start(f32[2,256,640]{2,1,0:T(8,128)} %slice.123), channel_id=1, source_target_pairs={{0,16},{4,20},{8,24},{12,28},{1,17},{5,21},{9,25},{13,29},{2,18},{... | collective-permute-start | bytes 3932168 | tf_op jit(solution)/shard_map/ppermute | solution.py:14
  116.6 4.0 %pad_maximum_fusion = f32[8,2,256,256]{2,3,0,1:T(8,128)} fusion(f32[8,1,256,256]{2,3,0,1:T(8,128)} %get-tuple-element.33, f32[8,1,256,256]{2,3,0,1:T(8,128)S(1)} %copy-done.2), kind=kLoop, calls=%fused_computation.1 | loop fusion | flops 1048576 | bytes 8388608 | tf_op jit(solution)/shard_map/stack | solution.py:81
  120.6 0.0 all-reduce.5.cloned.1.call-update
  120.7 0.0 all-reduce.3.cloned.1.call-start
  120.7 0.1 slice.121
  120.8 32.6 %collective-permute-done.2 = f32[2,256,640]{2,1,0:T(8,128)} collective-permute-done((f32[2,256,640]{2,1,0:T(8,128)}, f32[2,256,640]{2,1,0:T(8,128)}, u32[]{:S(2)}, u32[]{:S(2)}) %collective-permute-start.2) | collective-permute-done | bytes 1310752 | tf_op jit(solution)/shard_map/ppermute | solution.py:14
  153.4 1.5 fusion.13
  154.9 0.1 slice.126
  154.9 2.1 collective-permute-start.3
  157.0 0.1 slice_bitcast_fusion
  157.1 1.8 collective-permute-done.3
  158.9 0.1 fusion.19
  159.0 1.0 copy-done.3
  160.0 0.0 all-reduce.3.cloned.1.call-update
  160.0 107.2 %all-reduce.5.cloned.1.call-done = f32[8,2,256,256]{2,3,0,1:T(8,128)} async-done(((f32[8,2,256,256]{2,3,0,1:T(8,128)}), f32[8,2,256,256]{2,3,0,1:T(8,128)}) %all-reduce.5.cloned.1.call-update) | async-done | bytes 4194320 | tf_op jit(solution)/shard_map/psum | solution.py:90
  267.2 4.6 %broadcast_multiply_fusion = f32[8,2,256,256]{2,3,0,1:T(8,128)} fusion(f32[8,2,256,256]{2,3,0,1:T(8,128)} %all-reduce.5.cloned.1.call-done), kind=kLoop, calls=%fused_computation.18 | loop fusion | flops 1048576 | bytes 8388608 | tf_op jit(solution)/shard_map/div | solution.py:91
  271.8 5.4 %copy.20 = f32[8,2,256,256]{3,2,1,0:T(8,128)} copy(f32[8,2,256,256]{2,3,0,1:T(8,128)} %broadcast_multiply_fusion) | data formatting | bytes 8388608
  277.2 47.8 %all-reduce.3.cloned.1.call-done = f32[1,2,384,384]{3,2,1,0:T(8,128)} async-done(((f32[1,2,384,384]{3,2,1,0:T(8,128)}), f32[1,2,384,384]{3,2,1,0:T(8,128)}) %all-reduce.3.cloned.1.call-update) | async-done | bytes 1179664 | tf_op jit(solution)/shard_map/psum | solution.py:88
  325.0 2.4 copy.45
  (12 shorter events, 0.1 us)
Async XLA Ops:
  7.2 6.4 %copy-start.1 = (f32[1,2,384,384]{3,2,1,0:T(8,128)S(1)}, f32[1,2,384,384]{3,2,1,0:T(8,128)}, u32[]{:S(2)}) copy-start(f32[1,2,384,384]{3,2,1,0:T(8,128)} %param.8) | copy-start | bytes 3538948
  7.2 260.0 %all-reduce.5.cloned.1.call-start = ((), (), s32[]{:S(2)}) async-start(), calls=%async_computation.1 | async-start | bytes 8388608 | tf_op jit(solution)/shard_map/psum | solution.py:90
  7.2 8.8 %copy-start.5 = (s32[1,1,2]{2,1,0:T(1,128)S(1)}, s32[1,1,2]{2,1,0:T(1,128)}, u32[]{:S(2)}) copy-start(s32[1,1,2]{2,1,0:T(1,128)} %param.10) | copy-start | bytes 28
  8.5 4.2 %collective-permute-start = (f32[2,384,256]{2,1,0:T(8,128)S(1)}, f32[2,384,256]{2,1,0:T(8,128)S(1)}, u32[]{:S(2)}, u32[]{:S(2)}) collective-permute-start(f32[2,384,256]{2,1,0:T(8,128)S(1)} %slice.115), channel_id=1, source_target_pairs={{4,0},{8,4},{12,8},{16,12},{20,16},{24,20},{28,24},{5,1},{9,5},{13... | collective-permute-start | bytes 2359304 | tf_op jit(solution)/shard_map/ppermute | solution.py:14
  12.7 0.9 copy-start.4
  14.7 41.2 %collective-permute-start.1 = (f32[2,256,640]{2,1,0:T(8,128)}, f32[2,256,640]{2,1,0:T(8,128)}, u32[]{:S(2)}, u32[]{:S(2)}) collective-permute-start(f32[2,256,640]{2,1,0:T(8,128)} %pad_maximum_fusion.1), channel_id=1, source_target_pairs={{16,0},{20,4},{24,8},{28,12},{17,1},{21,5},{25,9},{29,13},{18,2},{... | collective-permute-start | bytes 3932168 | tf_op jit(solution)/shard_map/ppermute | solution.py:14
  92.5 7.2 %copy-start = (f32[8,2,256,256]{2,3,0,1:T(8,128)S(1)}, f32[8,2,256,256]{2,3,0,1:T(8,128)}, u32[]{:S(2)}) copy-start(f32[8,2,256,256]{2,3,0,1:T(8,128)} %convert_element_type.35) | copy-start | bytes 12582916
  111.0 5.6 %copy-start.2 = (f32[8,1,256,256]{2,3,0,1:T(8,128)S(1)}, f32[8,1,256,256]{2,3,0,1:T(8,128)}, u32[]{:S(2)}) copy-start(f32[8,1,256,256]{2,3,0,1:T(8,128)} %get-tuple-element.32) | copy-start | bytes 6291460
  112.2 41.2 %collective-permute-start.2 = (f32[2,256,640]{2,1,0:T(8,128)}, f32[2,256,640]{2,1,0:T(8,128)}, u32[]{:S(2)}, u32[]{:S(2)}) collective-permute-start(f32[2,256,640]{2,1,0:T(8,128)} %slice.123), channel_id=1, source_target_pairs={{0,16},{4,20},{8,24},{12,28},{1,17},{5,21},{9,25},{13,29},{2,18},{... | collective-permute-start | bytes 3932168 | tf_op jit(solution)/shard_map/ppermute | solution.py:14
  120.7 204.3 %all-reduce.3.cloned.1.call-start = ((), (), s32[]{:S(2)}) async-start(), calls=%async_computation | async-start | bytes 2359296 | tf_op jit(solution)/shard_map/psum | solution.py:88
  154.9 3.9 %collective-permute-start.3 = (f32[2,384,256]{2,1,0:T(8,128)S(1)}, f32[2,384,256]{2,1,0:T(8,128)S(1)}, u32[]{:S(2)}, u32[]{:S(2)}) collective-permute-start(f32[2,384,256]{2,1,0:T(8,128)S(1)} %slice.126), channel_id=1, source_target_pairs={{0,4},{4,8},{8,12},{12,16},{16,20},{20,24},{24,28},{1,5},{5,9},{9,... | collective-permute-start | bytes 2359304 | tf_op jit(solution)/shard_map/ppermute | solution.py:14
  159.0 1.0 copy-start.3
Sparse Core Ops, SparseCore 0:
  120.8 146.3 all-reduce.4
  270.1 54.7 all-reduce.2
where the time goes:
time: 339 us; the launch traced here: 334 us
  waiting for transfers between devices  219 us (65%)
  matrix products  38.9 us (11%)
  local copies, waits for them, and re-layouts  25.4 us (7%)
  other arithmetic  23.6 us (7%)
  between operations  18.3 us (5%)
  starting transfers between devices  9.15 us (3%)
    psum x1, waiting for transfers between devices, shards(): summed = lax.psum(grad_probe, ('tile', 'batch'))  107 us
    ppermute x4, waiting for transfers between devices, passed_along(): return lax.ppermute(block, axis, route)  64.1 us
    psum x1, waiting for transfers between devices, shards(): lax.psum(return_margins(grad_ext, tile_side, pattern), 'batch')  47.8 us
    dot_general x2, matrix products, transform(): jnp.einsum('ajbk,mbkc->majc', left_table, wave, precision=lax.Precision.H...  24.1 us
    dot_general x2, matrix products, transform(): jnp.einsum('mbjk,bkac->majc', half_done, right_table, precision=lax.Preci...  14.7 us
    unnamed x16, local copies, waits for them, and re-layouts  13.6 us
    ppermute x4, starting transfers between devices, passed_along(): return lax.ppermute(block, axis, route)  9.07 us
    dynamic_update_slice x1, local copies, waits for them, and re-layouts, shards(): lax.dynamic_update_slice(grad_ext, object_term, (zero_index, row_at, col_...  6.99 us
  transfers between devices with their start and end apart: 6, of which 6 were waited for; matrix products, arithmetic and copies ran while one was open for 7% of the time, Pallas kernels for 0%

commit v1 on v0

v1 whole, which is shorter than its diff:
```python
import functools
import math

import jax
import jax.numpy as jnp
import ml_dtypes
import numpy as np
from jax import lax
from jax.experimental import pallas as pl
from jax.experimental.pallas import tpu as pltpu
from jax.sharding import PartitionSpec as P

TILE_COLS = 4
MESH = pl.DeviceIdType.MESH
F32 = jnp.float32
BF16 = jnp.bfloat16


def split_table(table, axis):
    high = table.astype(np.float32).astype(ml_dtypes.bfloat16)
    low = (table - high.astype(np.float64)).astype(np.float32).astype(ml_dtypes.bfloat16)
    return np.concatenate([high, high, low], axis=axis)


def dft_tables(pattern):
    h = pattern // 2
    n, k = np.arange(h)[:, None], np.arange(h)[None, :]
    even = np.exp(-2j * np.pi * ((2 * n * k) % pattern) / pattern) / math.sqrt(pattern)
    odd = np.exp(-2j * np.pi * ((n * (2 * k + 1)) % pattern) / pattern) / math.sqrt(pattern)

    def right(m):
        return split_table(np.block([[m.real, m.imag], [-m.imag, m.real]]), 0)

    def left(m):
        return split_table(np.block([[m.real, -m.imag], [m.imag, m.real]]), 1)

    rights = np.stack([right(even), right(odd), right(even.conj().T), right(odd.conj().T)])
    lefts = np.stack([left(even.T), left(odd.T), left(even.conj()), left(odd.conj())])
    return rights, lefts


def split(x):
    high = x.astype(BF16)
    return high, (x - high.astype(F32)).astype(BF16)


def times_table(x, table):
    high, low = split(x)
    return jnp.dot(jnp.concatenate([high, low, high], 1), table, preferred_element_type=F32)


def table_times(table, x):
    high, low = split(x)
    return jnp.dot(table, jnp.concatenate([high, low, high], 0), preferred_element_type=F32)


def times_onehot(x, onehot):
    high, low = split(x)
    return jnp.dot(high, onehot, preferred_element_type=F32) + jnp.dot(
        low, onehot, preferred_element_type=F32
    )


def onehot_times(onehot, x):
    high, low = split(x)
    return jnp.dot(onehot, high, preferred_element_type=F32) + jnp.dot(
        onehot, low, preferred_element_type=F32
    )


def onehot(hit):
    return jnp.where(hit, 1.0, 0.0).astype(F32).astype(BF16)


def kernel(n_tile, n_batch, tile_ref, off_ref, amp_ref, probe_ref, right_ref, left_ref,
           og_ref, pg_ref, ext, patch, far, fac, ot, gext, acc, sendbuf, pairbuf, rsbuf, zbuf,
           objbuf, offbuf, xbuf, ybuf, send_sem, recv_sem):
    me = lax.axis_index("tile")
    z = lax.axis_index("batch")
    ts = tile_ref.shape[-1]
    modes, _, ps, _ = probe_ref.shape
    h = ps // 2
    mh = modes // 2
    bits = []
    b = 2
    while b < n_tile:
        bits.append(b)
        b *= 2
    core = lax.rem(me, 2)
    sibling = me + 1 - 2 * core
    col = lax.rem(me, TILE_COLS)
    has_left = col > 0
    has_right = col < TILE_COLS - 1
    has_up = me >= TILE_COLS
    has_down = me < n_tile - TILE_COLS
    count = [0]

    def sems(n=1):
        first = count[0]
        count[0] += n
        return first

    def remote(src, dst, sem, tile, batch):
        return pltpu.make_async_remote_copy(
            src_ref=src, dst_ref=dst, send_sem=send_sem.at[sem], recv_sem=recv_sem.at[sem],
            device_id=(tile, batch), device_id_type=MESH)

    barrier = pltpu.get_barrier_semaphore()

    def greet(tile, batch):
        pl.semaphore_signal(barrier, inc=1, device_id=(tile, batch), device_id_type=MESH)

    greet(sibling, z)
    for b in bits:
        greet(me + b * (1 - 2 * lax.rem(me // b, 2)), z)
    for d in range(1, n_batch):
        greet(me, lax.rem(z + d, n_batch))
    for there, step in ((has_left, -1), (has_right, 1), (has_up, -TILE_COLS), (has_down, TILE_COLS)):
        @pl.when(there)
        def _():
            greet(me + step, z)
    around = sum(jnp.where(t, 1, 0) for t in (has_left, has_right, has_up, has_down))
    pl.semaphore_wait(barrier, 1 + len(bits) + n_batch - 1 + around)

    up = [
        remote(tile_ref.at[:, :ps, :ps], ext.at[:, ts:, :ps], sems(), me - TILE_COLS, z),
        remote(tile_ref.at[:, :ps, ps:], ext.at[:, ts:, ps:ts], sems(), me - TILE_COLS, z),
    ]
    leftward = remote(tile_ref.at[:, :, :ps], ext.at[:, :ts, ts:], sems(), me - 1, z)
    corner = remote(ext.at[:, ts:, :ps], ext.at[:, ts:, ts:], sems(), me - 1, z)

    @pl.when(has_up)
    def _():
        up[0].start()
        up[1].start()

    @pl.when(has_left)
    def _():
        leftward.start()

    ext[:, :ts, :ts] = tile_ref[...]

    @pl.when(jnp.logical_not(has_right))
    def _():
        ext[:, :, ts:] = jnp.zeros((2, ts + ps, ps), F32)

    @pl.when(jnp.logical_not(has_down))
    def _():
        ext[:, ts:, :ts] = jnp.zeros((2, ps, ts), F32)

    @pl.when(jnp.logical_and(jnp.logical_not(has_down), has_right))
    def _():
        ext[:, ts:, ts:] = jnp.zeros((2, ps, ps), F32)

    rows = lax.broadcasted_iota(jnp.int32, (ps, ps), 0)
    cols = lax.broadcasted_iota(jnp.int32, (ps, ps), 1)
    by_row = onehot(cols == jnp.where(rows < h, 2 * rows, 2 * (rows - h) + 1))
    by_col = onehot(rows == jnp.where(cols < h, 2 * cols, 2 * (cols - h) + 1))
    fac[...] = times_onehot(onehot_times(by_row, amp_ref[...]), by_col)

    @pl.when(has_down)
    def _():
        up[0].wait_recv()

    @pl.when(jnp.logical_and(has_down, has_left))
    def _():
        corner.start()

    @pl.when(has_down)
    def _():
        up[1].wait_recv()

    @pl.when(has_right)
    def _():
        leftward.wait_recv()

    @pl.when(jnp.logical_and(has_down, has_right))
    def _():
        corner.wait_recv()

    r_at = off_ref[0:1, 0:1]
    c_at = off_ref[1:2, 0:1]
    te = ts + ps
    pick_r = onehot(lax.broadcasted_iota(jnp.int32, (ps, te), 1)
                    == lax.broadcasted_iota(jnp.int32, (ps, te), 0) + r_at)
    pick_c = onehot(lax.broadcasted_iota(jnp.int32, (te, ps), 0)
                    == lax.broadcasted_iota(jnp.int32, (te, ps), 1) + c_at)
    for part in range(2):
        patch[part] = times_onehot(onehot_times(pick_r, ext[part]), pick_c)

    @pl.when(has_up)
    def _():
        up[0].wait_send()
        up[1].wait_send()

    @pl.when(has_left)
    def _():
        leftward.wait_send()

    @pl.when(jnp.logical_and(has_down, has_left))
    def _():
        corner.wait_send()

    def forward(k, intensity):
        i0, i1 = intensity
        pr, pi = probe_ref[k, 0].astype(F32), probe_ref[k, 1].astype(F32)
        a, b = patch[0], patch[1]
        xr, xi = pr * a - pi * b, pr * b + pi * a
        plus = jnp.concatenate([xr[:, :h] + xr[:, h:], xi[:, :h] + xi[:, h:]], 1)
        minus = jnp.concatenate([xr[:, :h] - xr[:, h:], xi[:, :h] - xi[:, h:]], 1)
        e = times_table(plus, right_ref[0])
        o = times_table(minus, right_ref[1])
        re = jnp.concatenate([e[:, :h], o[:, :h]], 1)
        im = jnp.concatenate([e[:, h:], o[:, h:]], 1)
        g = table_times(left_ref[0], jnp.concatenate([re[:h] + re[h:], im[:h] + im[h:]], 0))
        f = table_times(left_ref[1], jnp.concatenate([re[:h] - re[h:], im[:h] - im[h:]], 0))
        far[k, 0] = g
        far[k, 1] = f
        return (i0 + g[:h] * g[:h] + g[h:] * g[h:], i1 + f[:h] * f[:h] + f[h:] * f[h:])

    zero = jnp.zeros((h, ps), F32)
    i0, i1 = lax.fori_loop(0, modes, forward, (zero, zero))
    fac[:h] = 1.0 - fac[:h] / jnp.sqrt(i0 + 0.01)
    fac[h:] = 1.0 - fac[h:] / jnp.sqrt(i1 + 0.01)
    ot[...] = jnp.zeros_like(ot)

    def backward(k):
        f0, f1 = fac[:h], fac[h:]
        g = far[k, 0] * jnp.concatenate([f0, f0], 0)
        f = far[k, 1] * jnp.concatenate([f1, f1], 0)
        p = table_times(left_ref[2], g)
        q = table_times(left_ref[3], f)
        top, low = p + q, p - q
        re = jnp.concatenate([top[:h], low[:h]], 0)
        im = jnp.concatenate([top[h:], low[h:]], 0)
        e = times_table(jnp.concatenate([re[:, :h], im[:, :h]], 1), right_ref[2])
        o = times_table(jnp.concatenate([re[:, h:], im[:, h:]], 1), right_ref[3])
        br = jnp.concatenate([e[:, :h] + o[:, :h], e[:, :h] - o[:, :h]], 1)
        bi = jnp.concatenate([e[:, h:] + o[:, h:], e[:, h:] - o[:, h:]], 1)
        pr, pi = probe_ref[k, 0].astype(F32), probe_ref[k, 1].astype(F32)
        ot[0] += pr * br + pi * bi
        ot[1] += pr * bi - pi * br
        a, b = patch[0], patch[1]
        return a * br + b * bi, a * bi - b * br

    mode_rows = 2 * ps
    pair = sems(mh)

    def pair_copy(i):
        at = pl.ds(pl.multiple_of(i * mode_rows, mode_rows), mode_rows)
        return remote(sendbuf.at[at], pairbuf.at[at], pair + i, sibling, z)

    def for_sibling(i, carry):
        gr, gi = backward((1 - core) * mh + i)
        at = pl.multiple_of(i * mode_rows, mode_rows)
        sendbuf[pl.ds(at, ps)] = gr
        sendbuf[pl.ds(at + ps, ps)] = gi
        pair_copy(i).start()
        return carry

    lax.fori_loop(0, mh, for_sibling, 0)

    def for_self(i, carry):
        gr, gi = backward(core * mh + i)
        pair_copy(i).wait_recv()
        at = pl.multiple_of(i * mode_rows, mode_rows)
        acc[pl.ds(at, ps)] = gr + pairbuf[pl.ds(at, ps)]
        acc[pl.ds(at + ps, ps)] = gi + pairbuf[pl.ds(at + ps, ps)]
        return carry

    length = mh * mode_rows // 2
    base_out = core * (mh * mode_rows)

    class Stream:
        def __init__(self, index, order):
            self.index, self.order = index, order
            self.first = index * length
            self.start, self.size, self.step = self.first, length, 0
            self.slot = 0
            self.sem_rs = sems(len(order))
            self.sem_ag = sems(len(order))
            self.sem_z = sems(n_batch)
            self.sem_zg = sems(n_batch)
            self.sem_pair = sems()
            self.trail = []

        def rows(self, at, n):
            return pl.ds(pl.multiple_of(at, n), n)

        def rs_start(self):
            b = self.order[self.step]
            mine = lax.rem(me // b, 2)
            half = self.size // 2
            self.partner = me + b * (1 - 2 * mine)
            self.trail.append((self.start, self.size, self.partner, mine))
            self.copy = remote(
                acc.at[self.rows(self.start + (1 - mine) * half, half)],
                rsbuf.at[self.index, pl.ds(self.slot, half)],
                self.sem_rs + self.step, self.partner, z)
            self.copy.start()
            self.start = self.start + mine * half
            self.size = half

        def rs_wait(self):
            self.copy.wait()
            at = self.rows(self.start, self.size)
            acc[at] += rsbuf[self.index, self.slot:self.slot + self.size]
            self.slot += self.size
            self.step += 1

        def z_start(self):
            q = self.size // n_batch
            self.q = q
            self.copies = []
            for d in range(1, n_batch):
                dest = lax.rem(z + d, n_batch)
                c = remote(acc.at[self.rows(self.start + dest * q, q)], zbuf.at[self.index, d],
                           self.sem_z + d, me, dest)
                c.start()
                self.copies.append(c)

        def z_wait(self):
            for c in self.copies:
                c.wait()
            total = acc[self.rows(self.start + z * self.q, self.q)]
            for d in range(1, n_batch):
                total = total + zbuf[self.index, d]
            at = self.rows(base_out + self.start + z * self.q, self.q)
            pg_ref[at] = total
            self.copies = []
            for d in range(1, n_batch):
                c = remote(pg_ref.at[at], pg_ref.at[at], self.sem_zg + d, me, lax.rem(z + d, n_batch))
                c.start()
                self.copies.append(c)

        def zg_wait(self):
            for c in self.copies:
                c.wait()

        def ag_start(self):
            self.step -= 1
            start, size, partner, mine = self.trail[self.step]
            at = self.rows(base_out + start + mine * (size // 2), size // 2)
            self.copy = remote(pg_ref.at[at], pg_ref.at[at], self.sem_ag + self.step, partner, z)
            self.copy.start()

        def ag_wait(self):
            self.copy.wait()

        def pair_start(self):
            at = self.rows(base_out + self.first, length)
            self.copy = remote(pg_ref.at[at], pg_ref.at[at], self.sem_pair, sibling, z)
            self.copy.start()

    streams = [Stream(0, bits), Stream(1, bits[::-1])]

    lax.fori_loop(0, mh // 2, for_self, 0)
    streams[0].rs_start()
    lax.fori_loop(mh // 2, mh, for_self, 0)
    streams[1].rs_start()

    osem, fsem = sems(n_batch), sems(n_batch)
    objects = []
    for d in range(1, n_batch):
        dest = lax.rem(z + d, n_batch)
        objects.append(remote(off_ref, offbuf.at[d], fsem + d, me, dest))
        objects.append(remote(ot, objbuf.at[d], osem + d, me, dest))
    for c in objects:
        c.start()

    for step in range(len(bits)):
        for s in streams:
            s.rs_wait()
            if step + 1 < len(bits):
                s.rs_start()
            else:
                s.z_start()

    for c in objects:
        c.wait()
    right_sem, down_sem = sems(2), sems(2)
    rightward, downward = [], []
    for part in range(2):
        total = None
        for d in range(n_batch):
            offs = off_ref if d == 0 else offbuf.at[d]
            term = ot[part] if d == 0 else objbuf[d, part]
            put_r = onehot(lax.broadcasted_iota(jnp.int32, (te, ps), 0)
                           == lax.broadcasted_iota(jnp.int32, (te, ps), 1) + offs[0:1, 0:1])
            put_c = onehot(lax.broadcasted_iota(jnp.int32, (ps, te), 1)
                           == lax.broadcasted_iota(jnp.int32, (ps, te), 0) + offs[1:2, 0:1])
            if d == 0:
                gext[part] = times_onehot(onehot_times(put_r, term), put_c)
            else:
                gext[part] += times_onehot(onehot_times(put_r, term), put_c)
        c = remote(gext.at[part, :, ts:], xbuf.at[part], right_sem + part, me + 1, z)
        rightward.append(c)

        @pl.when(has_right)
        def _():
            c.start()

    for s in streams:
        s.z_wait()

    for part in range(2):
        @pl.when(has_left)
        def _():
            rightward[part].wait_recv()
            gext[part, :, :ps] += xbuf[part]

        c = remote(gext.at[part, ts:, :ts], ybuf.at[part], down_sem + part, me + TILE_COLS, z)
        downward.append(c)

        @pl.when(has_down)
        def _():
            c.start()

    for s in streams:
        s.zg_wait()
        s.ag_start()
    for step in range(len(bits)):
        for s in streams:
            s.ag_wait()
            if step + 1 < len(bits):
                s.ag_start()
            else:
                s.pair_start()

    for part in range(2):
        og_ref[part] = gext[part, :ts, :ts]

        @pl.when(has_up)
        def _():
            downward[part].wait_recv()
            og_ref[part, :ps, :] += ybuf[part]

    for part in range(2):
        @pl.when(has_right)
        def _():
            rightward[part].wait_send()

        @pl.when(has_down)
        def _():
            downward[part].wait_send()

    for s in streams:
        s.copy.wait()

    def sent(i, carry):
        pair_copy(i).wait_send()
        return carry

    lax.fori_loop(0, mh, sent, 0)


def n_sems(n_tile, n_batch, modes):
    n_bits = n_tile.bit_length() - 2
    return 4 + modes // 2 + 2 * (2 * n_bits + 2 * n_batch + 1) + 2 * n_batch + 4


def shards(n_tile, n_batch, object_tiles, probe, offsets, amplitude):
    modes, _, ps, _ = probe.shape
    ts = object_tiles.shape[-1]
    te = ts + ps
    rights, lefts = dft_tables(ps)
    held = jnp.broadcast_to(jnp.pad(offsets[0, 0], (0, 6))[:, None], (8, 128))
    n = n_sems(n_tile, n_batch, modes)
    half = modes // 2 * 2 * ps
    quarter = half // 2
    q = quarter // (n_tile // 2) // n_batch
    vmem = pl.BlockSpec(memory_space=pltpu.VMEM)
    og, pg = pl.pallas_call(
        functools.partial(kernel, n_tile, n_batch),
        out_shape=(jax.ShapeDtypeStruct((2, ts, ts), F32),
                   jax.ShapeDtypeStruct((modes * 2 * ps, ps), F32)),
        in_specs=[vmem] * 6,
        out_specs=(vmem, vmem),
        scratch_shapes=[
            pltpu.VMEM((2, te, te), F32),
            pltpu.VMEM((2, ps, ps), F32),
            pltpu.VMEM((modes, 2, ps, ps), F32),
            pltpu.VMEM((ps, ps), F32),
            pltpu.VMEM((2, ps, ps), F32),
            pltpu.VMEM((2, te, te), F32),
            pltpu.VMEM((half, ps), F32),
            pltpu.VMEM((half, ps), F32),
            pltpu.VMEM((half, ps), F32),
            pltpu.VMEM((2, quarter, ps), F32),
            pltpu.VMEM((2, n_batch, q, ps), F32),
            pltpu.VMEM((n_batch, 2, ps, ps), F32),
            pltpu.VMEM((n_batch, 8, 128), jnp.int32),
            pltpu.VMEM((2, te, ps), F32),
            pltpu.VMEM((2, ps, ts), F32),
            pltpu.SemaphoreType.DMA((n,)),
            pltpu.SemaphoreType.DMA((n,)),
        ],
        compiler_params=pltpu.CompilerParams(
            collective_id=0, has_side_effects=True, vmem_limit_bytes=56 * 1024 * 1024),
        cost_estimate=pl.CostEstimate(flops=13_000_000_000, bytes_accessed=20_000_000, transcendentals=0),
        name="ptycho",
    )(object_tiles[0], held, amplitude[0, 0], probe, rights, lefts)
    positions = n_tile * n_batch * offsets.shape[1]
    return og[None], pg.reshape(modes, 2, ps, ps) * (1.0 / math.sqrt(positions))


def solution(mesh):
    placed = (
        P("tile", None, None, None),
        P(),
        P("tile", "batch", None),
        P("tile", "batch", None, None),
    )
    return jax.shard_map(
        functools.partial(shards, mesh.shape["tile"], mesh.shape["batch"]),
        mesh=mesh,
        in_specs=placed,
        out_specs=(P("tile", None, None, None), P()),
        check_vma=False,
    )
```

time: 339 us -> 154 us (0.45)
  waiting for transfers between devices: 219 us -> 0 us
  Pallas kernels: 0 us -> 144 us
  matrix products: 38.9 us -> 0 us
  local copies, waits for them, and re-layouts: 25.4 us -> 2.34 us
  other arithmetic: 23.6 us -> 4.66 us
  between operations: 18.3 us -> 0.65 us
  starting transfers between devices: 9.15 us -> 0 us
    psum x2 -> x0, waiting for transfers between devices: 155 us -> none  [the longest x1 107 us: shards(): summed = lax.psum(grad_probe, ('tile', 'batch'))]
    pallas_call x0 -> x1, Pallas kernels: none -> 144 us  [shards(): pl.pallas_call(functools.partial(kernel, n_tile, n_batch), out_shape=(jax...]
    ppermute x4 -> x0, waiting for transfers between devices: 64.1 us -> none  [passed_along(): return lax.ppermute(block, axis, route)]
    dot_general x4 -> x0, matrix products: 38.9 us -> none  [the longest x2 24.1 us: transform(): jnp.einsum('ajbk,mbkc->majc', left_table, wave, precision=lax.Precision.H...]
    unnamed x16 -> x3, local copies, waits for them, and re-layouts: 13.6 us -> 1.02 us
    ppermute x4 -> x0, starting transfers between devices: 9.07 us -> none  [passed_along(): return lax.ppermute(block, axis, route)]
    dynamic_update_slice x1 -> x0, local copies, waits for them, and re-layouts: 6.99 us -> none  [shards(): lax.dynamic_update_slice(grad_ext, object_term, (zero_index, row_at, col_...]
    div x2 -> x0, other arithmetic: 5.65 us -> none  [the longest x1 4.59 us: shards(): return (object_grad[None], summed / math.sqrt(positions))]
  transfers between devices with their start and end apart: 6 -> 0, of which waited for: 6 -> 0; matrix products, arithmetic and copies ran while one was open for 7% -> 0% of each run, Pallas kernels for 0% -> 0%
where the time goes in v1:
time: 154 us; the launch traced here: 152 us
  Pallas kernels  144 us (94%)
  other arithmetic  4.66 us (3%)
  local copies, waits for them, and re-layouts  2.34 us (2%)
    pallas_call x1, Pallas kernels, shards(): pl.pallas_call(functools.partial(kernel, n_tile, n_batch), out_shape=(jax...  144 us
    mul x1, other arithmetic, shards(): pg.reshape(modes, 2, ps, ps) * (1.0 / math.sqrt(positions))  4.66 us

profile of v1, /device:TPU:0, one launch (start us, length us, event | category | flops | bytes accessed | tf_op | source)
XLA Modules:
  0.0 151.9 jit_solution(10763875050364616964)
XLA Ops:
  0.6 0.7 pad.4
  1.3 0.7 broadcast_in_dim.4.off_ref
  2.0 144.2 %ptycho.1 = (f32[2,384,384]{2,1,0:T(8,128)}, f32[4096,256]{1,0:T(8,128)}) custom-call(f32[2,384,384]{2,1,0:T(8,128)} %bitcast.7, s32[8,128]{1,0:T(8,128)} %broadcast_in_dim.4.off_ref, f32[256,256]{1,0:T(8,128)} %bitcast.8, bf16[8,2,256,256]{3,2,1,0:T(8,128)(2,1)} %probe_ref.1, bf16[4,768,256]{2,1,0:T(8,128)(2,1)} %constant.8.clone.right_ref, ...), custom_call_target="tpu_custom_call" | custom-call | flops 12999999488 | bytes 20000000 | tf_op jit(solution)/shard_map/ptycho/pallas_call | solution.py:473
  146.2 0.0 copy-start
  146.2 4.7 %broadcast_multiply_fusion = f32[4096,256]{1,0:T(8,128)} fusion(f32[4096,256]{1,0:T(8,128)} %get-tuple-element.5), kind=kLoop, calls=%fused_computation | loop fusion | flops 1048576 | bytes 8388608 | tf_op jit(solution)/shard_map/mul | solution.py:504
  150.9 0.0 copy-done
  150.9 1.0 copy.9
Async XLA Ops:
  146.2 4.7 %copy-start = (f32[2,384,384]{2,1,0:T(8,128)S(1)}, f32[2,384,384]{2,1,0:T(8,128)}, u32[]{:S(2)}) copy-start(f32[2,384,384]{2,1,0:T(8,128)} %get-tuple-element.4) | copy-start | bytes 3538948

commit v2 on v1

--- a/solution.py
+++ b/solution.py
@@ -122,6 +122,12 @@
     around = sum(jnp.where(t, 1, 0) for t in (has_left, has_right, has_up, has_down))
     pl.semaphore_wait(barrier, 1 + len(bits) + n_batch - 1 + around)
 
+    fsem = sems(n_batch)
+    offs_out = [remote(off_ref, offbuf.at[d], fsem + d, me, lax.rem(z + d, n_batch))
+                for d in range(1, n_batch)]
+    for c in offs_out:
+        c.start()
+
     up = [
         remote(tile_ref.at[:, :ps, :ps], ext.at[:, ts:, :ps], sems(), me - TILE_COLS, z),
         remote(tile_ref.at[:, :ps, ps:], ext.at[:, ts:, ps:ts], sems(), me - TILE_COLS, z),
@@ -219,7 +225,8 @@
         return (i0 + g[:h] * g[:h] + g[h:] * g[h:], i1 + f[:h] * f[:h] + f[h:] * f[h:])
 
     zero = jnp.zeros((h, ps), F32)
-    i0, i1 = lax.fori_loop(0, modes, forward, (zero, zero))
+    i0, i1 = lax.fori_loop(
+        0, modes // 2, lambda i, c: forward(2 * i + 1, forward(2 * i, c)), (zero, zero))
     fac[:h] = 1.0 - fac[:h] / jnp.sqrt(i0 + 0.01)
     fac[h:] = 1.0 - fac[h:] / jnp.sqrt(i1 + 0.01)
     ot[...] = jnp.zeros_like(ot)
@@ -250,25 +257,21 @@
         at = pl.ds(pl.multiple_of(i * mode_rows, mode_rows), mode_rows)
         return remote(sendbuf.at[at], pairbuf.at[at], pair + i, sibling, z)
 
-    def for_sibling(i, carry):
+    def both(i):
         gr, gi = backward((1 - core) * mh + i)
         at = pl.multiple_of(i * mode_rows, mode_rows)
         sendbuf[pl.ds(at, ps)] = gr
         sendbuf[pl.ds(at + ps, ps)] = gi
         pair_copy(i).start()
-        return carry
-
-    lax.fori_loop(0, mh, for_sibling, 0)
-
-    def for_self(i, carry):
         gr, gi = backward(core * mh + i)
         pair_copy(i).wait_recv()
-        at = pl.multiple_of(i * mode_rows, mode_rows)
         acc[pl.ds(at, ps)] = gr + pairbuf[pl.ds(at, ps)]
         acc[pl.ds(at + ps, ps)] = gi + pairbuf[pl.ds(at + ps, ps)]
-        return carry
-
-    length = mh * mode_rows // 2
+
+    n_streams = streams_of(n_tile, n_batch, mh, mode_rows)
+    length = mh * mode_rows // n_streams
+    per_stream = mh // n_streams
+    stream_sems = 2 * len(bits) + 2 * n_batch + 1
     base_out = core * (mh * mode_rows)
 
     class Stream:
@@ -277,11 +280,11 @@
             self.first = index * length
             self.start, self.size, self.step = self.first, length, 0
             self.slot = 0
-            self.sem_rs = sems(len(order))
-            self.sem_ag = sems(len(order))
-            self.sem_z = sems(n_batch)
-            self.sem_zg = sems(n_batch)
-            self.sem_pair = sems()
+            self.sem_rs = stream_base + index * stream_sems
+            self.sem_ag = self.sem_rs + len(order)
+            self.sem_z = self.sem_ag + len(order)
+            self.sem_zg = self.sem_z + n_batch
+            self.sem_pair = self.sem_zg + n_batch
             self.trail = []
 
         def rows(self, at, n):
@@ -297,7 +300,8 @@
                 acc.at[self.rows(self.start + (1 - mine) * half, half)],
                 rsbuf.at[self.index, pl.ds(self.slot, half)],
                 self.sem_rs + self.step, self.partner, z)
-            self.copy.start()
+            if self.step:
+                self.copy.start()
             self.start = self.start + mine * half
             self.size = half
 
@@ -352,21 +356,81 @@
             self.copy = remote(pg_ref.at[at], pg_ref.at[at], self.sem_pair, sibling, z)
             self.copy.start()
 
-    streams = [Stream(0, bits), Stream(1, bits[::-1])]
-
-    lax.fori_loop(0, mh // 2, for_self, 0)
-    streams[0].rs_start()
-    lax.fori_loop(mh // 2, mh, for_self, 0)
-    streams[1].rs_start()
-
-    osem, fsem = sems(n_batch), sems(n_batch)
-    objects = []
-    for d in range(1, n_batch):
-        dest = lax.rem(z + d, n_batch)
-        objects.append(remote(off_ref, offbuf.at[d], fsem + d, me, dest))
-        objects.append(remote(ot, objbuf.at[d], osem + d, me, dest))
-    for c in objects:
-        c.start()
+    stream_base = sems(n_streams * stream_sems)
+
+    def summed(i, carry):
+        for j in range(per_stream):
+            both(i * per_stream + j)
+        bit = bits[0] + lax.rem(i, 2) * (bits[-1] - bits[0])
+        mine = lax.rem(me // bit, 2)
+        half = length // 2
+        at = pl.multiple_of(i * length + (1 - mine) * half, half)
+        remote(acc.at[pl.ds(at, half)], rsbuf.at[i, pl.ds(0, half)],
+               stream_base + i * stream_sems, me + bit * (1 - 2 * mine), z).start()
+        return carry
+
+    lax.fori_loop(0, n_streams, summed, 0)
+    streams = [Stream(i, bits if i % 2 == 0 else bits[::-1]) for i in range(n_streams)]
+    for s in streams:
+        s.rs_start()
+
+    osem = sems(2 * n_batch)
+
+    def passing(way, stage):
+        origin = z - way * stage
+        sends = jnp.logical_and(
+            jnp.logical_and(origin >= 0, origin < n_batch),
+            jnp.logical_and(z + way >= 0, z + way < n_batch))
+        at = jnp.clip(origin, 0, n_batch - 1)
+        src = ot if stage == 0 else objbuf.at[at]
+        to = jnp.clip(z + way, 0, n_batch - 1)
+        return sends, remote(src, objbuf.at[at], osem + stage + (n_batch if way < 0 else 0), me, to)
+
+    def arrival(way, stage):
+        origin = z - way * (1 + stage)
+        comes = jnp.logical_and(origin >= 0, origin < n_batch)
+        at = jnp.clip(origin, 0, n_batch - 1)
+        return comes, at, remote(ot, objbuf.at[at], osem + stage + (n_batch if way < 0 else 0),
+                                 me, jnp.clip(z + way, 0, n_batch - 1))
+
+    def start_passing(stage):
+        for way in (1, -1):
+            sends, c = passing(way, stage)
+
+            @pl.when(sends)
+            def _():
+                c.start()
+
+    def place(offs, term, part):
+        put_r = onehot(lax.broadcasted_iota(jnp.int32, (te, ps), 0)
+                       == lax.broadcasted_iota(jnp.int32, (te, ps), 1) + offs[0:1, 0:1])
+        put_c = onehot(lax.broadcasted_iota(jnp.int32, (ps, te), 1)
+                       == lax.broadcasted_iota(jnp.int32, (ps, te), 0) + offs[1:2, 0:1])
+        return onehot_times(put_r, times_onehot(term, put_c))
+
+    def arrived(stage):
+        for way in (1, -1):
+            comes, at, c = arrival(way, stage)
+
+            @pl.when(comes)
+            def _():
+                c.wait_recv()
+        if stage + 1 < n_batch - 1:
+            start_passing(stage + 1)
+        for way in (1, -1):
+            comes, at, c = arrival(way, stage)
+            slot = stage + 1 if way > 0 else n_batch - 1 - stage
+
+            @pl.when(comes)
+            def _():
+                for part in range(2):
+                    gext[part] += place(offbuf.at[slot], objbuf[at, part], part)
+
+    start_passing(0)
+    for part in range(2):
+        gext[part] = place(off_ref, ot[part], part)
+    for c in offs_out:
+        c.wait()
 
     for step in range(len(bits)):
         for s in streams:
@@ -376,23 +440,11 @@
             else:
                 s.z_start()
 
-    for c in objects:
-        c.wait()
+    for stage in range(n_batch - 1):
+        arrived(stage)
     right_sem, down_sem = sems(2), sems(2)
     rightward, downward = [], []
     for part in range(2):
-        total = None
-        for d in range(n_batch):
-            offs = off_ref if d == 0 else offbuf.at[d]
-            term = ot[part] if d == 0 else objbuf[d, part]
-            put_r = onehot(lax.broadcasted_iota(jnp.int32, (te, ps), 0)
-                           == lax.broadcasted_iota(jnp.int32, (te, ps), 1) + offs[0:1, 0:1])
-            put_c = onehot(lax.broadcasted_iota(jnp.int32, (ps, te), 1)
-                           == lax.broadcasted_iota(jnp.int32, (ps, te), 0) + offs[1:2, 0:1])
-            if d == 0:
-                gext[part] = times_onehot(onehot_times(put_r, term), put_c)
-            else:
-                gext[part] += times_onehot(onehot_times(put_r, term), put_c)
         c = remote(gext.at[part, :, ts:], xbuf.at[part], right_sem + part, me + 1, z)
         rightward.append(c)
 
@@ -447,6 +499,14 @@
     for s in streams:
         s.copy.wait()
 
+    for stage in range(n_batch - 1):
+        for way in (1, -1):
+            sends, c = passing(way, stage)
+
+            @pl.when(sends)
+            def _():
+                c.wait_send()
+
     def sent(i, carry):
         pair_copy(i).wait_send()
         return carry
@@ -454,9 +514,13 @@
     lax.fori_loop(0, mh, sent, 0)
 
 
-def n_sems(n_tile, n_batch, modes):
+def streams_of(n_tile, n_batch, mh, mode_rows):
+    return mh if mode_rows // (n_tile // 2) // n_batch >= 8 else 2
+
+
+def n_sems(n_tile, n_batch, mh, n_streams):
     n_bits = n_tile.bit_length() - 2
-    return 4 + modes // 2 + 2 * (2 * n_bits + 2 * n_batch + 1) + 2 * n_batch + 4
+    return 4 + mh + n_streams * (2 * n_bits + 2 * n_batch + 1) + 3 * n_batch + 4
 
 
 def shards(n_tile, n_batch, object_tiles, probe, offsets, amplitude):
@@ -465,10 +529,11 @@
     te = ts + ps
     rights, lefts = dft_tables(ps)
     held = jnp.broadcast_to(jnp.pad(offsets[0, 0], (0, 6))[:, None], (8, 128))
-    n = n_sems(n_tile, n_batch, modes)
+    n_streams = streams_of(n_tile, n_batch, modes // 2, 2 * ps)
+    n = n_sems(n_tile, n_batch, modes // 2, n_streams)
     half = modes // 2 * 2 * ps
-    quarter = half // 2
-    q = quarter // (n_tile // 2) // n_batch
+    length = half // n_streams
+    q = length // (n_tile // 2) // n_batch
     vmem = pl.BlockSpec(memory_space=pltpu.VMEM)
     og, pg = pl.pallas_call(
         functools.partial(kernel, n_tile, n_batch),
@@ -486,8 +551,8 @@
             pltpu.VMEM((half, ps), F32),
             pltpu.VMEM((half, ps), F32),
             pltpu.VMEM((half, ps), F32),
-            pltpu.VMEM((2, quarter, ps), F32),
-            pltpu.VMEM((2, n_batch, q, ps), F32),
+            pltpu.VMEM((n_streams, length, ps), F32),
+            pltpu.VMEM((n_streams, n_batch, q, ps), F32),
             pltpu.VMEM((n_batch, 2, ps, ps), F32),
             pltpu.VMEM((n_batch, 8, 128), jnp.int32),
             pltpu.VMEM((2, te, ps), F32),

time: 154 us -> 153 us (level); the launches traced: 152 us -> 153 us
  no operation moved by 1% of the time
where the time goes in v2:
time: 153 us
  Pallas kernels  145 us (95%)
  other arithmetic  4.66 us (3%)
  local copies, waits for them, and re-layouts  2.34 us (2%)
    pallas_call x1, Pallas kernels, shards(): pl.pallas_call(functools.partial(kernel, n_tile, n_batch), out_shape=(jax...  145 us
    mul x1, other arithmetic, shards(): pg.reshape(modes, 2, ps, ps) * (1.0 / math.sqrt(positions))  4.66 us

profile of v2, /device:TPU:0, one launch (start us, length us, event | category | flops | bytes accessed | tf_op | source)
XLA Modules:
  0.0 152.9 jit_solution(13228140209874165989)
XLA Ops:
  0.6 0.7 pad.4
  1.3 0.7 broadcast_in_dim.4.off_ref
  2.0 145.2 %ptycho.1 = (f32[2,384,384]{2,1,0:T(8,128)}, f32[4096,256]{1,0:T(8,128)}) custom-call(f32[2,384,384]{2,1,0:T(8,128)} %bitcast.7, s32[8,128]{1,0:T(8,128)} %broadcast_in_dim.4.off_ref, f32[256,256]{1,0:T(8,128)} %bitcast.8, bf16[8,2,256,256]{3,2,1,0:T(8,128)(2,1)} %probe_ref.1, bf16[4,768,256]{2,1,0:T(8,128)(2,1)} %constant.8.clone.right_ref, ...), custom_call_target="tpu_custom_call" | custom-call | flops 12999999488 | bytes 20000000 | tf_op jit(solution)/shard_map/ptycho/pallas_call | solution.py:538
  147.2 0.0 copy-start
  147.2 4.7 %broadcast_multiply_fusion = f32[4096,256]{1,0:T(8,128)} fusion(f32[4096,256]{1,0:T(8,128)} %get-tuple-element.5), kind=kLoop, calls=%fused_computation | loop fusion | flops 1048576 | bytes 8388608 | tf_op jit(solution)/shard_map/mul | solution.py:569
  151.9 0.0 copy-done
  151.9 1.0 copy.9
Async XLA Ops:
  147.2 4.7 %copy-start = (f32[2,384,384]{2,1,0:T(8,128)S(1)}, f32[2,384,384]{2,1,0:T(8,128)}, u32[]{:S(2)}) copy-start(f32[2,384,384]{2,1,0:T(8,128)} %get-tuple-element.4) | copy-start | bytes 3538948

commit v3 on v2

--- a/solution.py
+++ b/solution.py
@@ -374,103 +374,116 @@
     for s in streams:
         s.rs_start()
 
-    osem = sems(2 * n_batch)
-
-    def passing(way, stage):
+    osem = sems(4 * n_batch)
+    hops = n_batch - 1
+
+    def sem_of(way, stage, part):
+        return osem + stage + n_batch * (2 * part + (1 if way < 0 else 0))
+
+    def passing(way, stage, part):
         origin = z - way * stage
         sends = jnp.logical_and(
             jnp.logical_and(origin >= 0, origin < n_batch),
             jnp.logical_and(z + way >= 0, z + way < n_batch))
         at = jnp.clip(origin, 0, n_batch - 1)
-        src = ot if stage == 0 else objbuf.at[at]
+        src = ot.at[part] if stage == 0 else objbuf.at[at, part]
         to = jnp.clip(z + way, 0, n_batch - 1)
-        return sends, remote(src, objbuf.at[at], osem + stage + (n_batch if way < 0 else 0), me, to)
-
-    def arrival(way, stage):
+        return sends, remote(src, objbuf.at[at, part], sem_of(way, stage, part), me, to)
+
+    def arrival(way, stage, part):
         origin = z - way * (1 + stage)
         comes = jnp.logical_and(origin >= 0, origin < n_batch)
         at = jnp.clip(origin, 0, n_batch - 1)
-        return comes, at, remote(ot, objbuf.at[at], osem + stage + (n_batch if way < 0 else 0),
+        return comes, at, remote(ot.at[part], objbuf.at[at, part], sem_of(way, stage, part),
                                  me, jnp.clip(z + way, 0, n_batch - 1))
 
-    def start_passing(stage):
+    def start_passing(stage, part):
         for way in (1, -1):
-            sends, c = passing(way, stage)
+            sends, c = passing(way, stage, part)
 
             @pl.when(sends)
             def _():
                 c.start()
 
-    def place(offs, term, part):
+    def place(offs, term):
         put_r = onehot(lax.broadcasted_iota(jnp.int32, (te, ps), 0)
                        == lax.broadcasted_iota(jnp.int32, (te, ps), 1) + offs[0:1, 0:1])
         put_c = onehot(lax.broadcasted_iota(jnp.int32, (ps, te), 1)
                        == lax.broadcasted_iota(jnp.int32, (ps, te), 0) + offs[1:2, 0:1])
         return onehot_times(put_r, times_onehot(term, put_c))
 
-    def arrived(stage):
+    right_sem, down_sem = sems(2), sems(2)
+    rightward = [remote(gext.at[part, :, ts:], xbuf.at[part], right_sem + part, me + 1, z)
+                 for part in range(2)]
+    downward = [remote(gext.at[part, ts:, :ts], ybuf.at[part], down_sem + part, me + TILE_COLS, z)
+                for part in range(2)]
+
+    def arrived(stage, part):
         for way in (1, -1):
-            comes, at, c = arrival(way, stage)
+            comes, at, c = arrival(way, stage, part)
 
             @pl.when(comes)
             def _():
                 c.wait_recv()
-        if stage + 1 < n_batch - 1:
-            start_passing(stage + 1)
+        if stage + 1 < hops:
+            start_passing(stage + 1, part)
+        if part == 0 and stage == max(hops - 2, 0):
+            start_passing(0, 1)
         for way in (1, -1):
-            comes, at, c = arrival(way, stage)
+            comes, at, c = arrival(way, stage, part)
             slot = stage + 1 if way > 0 else n_batch - 1 - stage
 
             @pl.when(comes)
             def _():
-                for part in range(2):
-                    gext[part] += place(offbuf.at[slot], objbuf[at, part], part)
-
-    start_passing(0)
+                gext[part] += place(offbuf.at[slot], objbuf[at, part])
+
+        if stage + 1 == hops:
+            @pl.when(has_right)
+            def _():
+                rightward[part].start()
+
+    def margin(part):
+        @pl.when(has_left)
+        def _():
+            rightward[part].wait_recv()
+            gext[part, :, :ps] += xbuf[part]
+
+        @pl.when(has_down)
+        def _():
+            downward[part].start()
+
+    start_passing(0, 0)
     for part in range(2):
-        gext[part] = place(off_ref, ot[part], part)
+        gext[part] = place(off_ref, ot[part])
     for c in offs_out:
         c.wait()
 
+    todo = [functools.partial(arrived, stage, part) for part in range(2) for stage in range(hops)]
+
+    def serve():
+        if todo:
+            todo.pop(0)()
+
     for step in range(len(bits)):
+        serve()
         for s in streams:
             s.rs_wait()
             if step + 1 < len(bits):
                 s.rs_start()
             else:
                 s.z_start()
-
-    for stage in range(n_batch - 1):
-        arrived(stage)
-    right_sem, down_sem = sems(2), sems(2)
-    rightward, downward = [], []
-    for part in range(2):
-        c = remote(gext.at[part, :, ts:], xbuf.at[part], right_sem + part, me + 1, z)
-        rightward.append(c)
-
-        @pl.when(has_right)
-        def _():
-            c.start()
-
+    while len(todo) > hops:
+        serve()
+    serve()
     for s in streams:
         s.z_wait()
-
-    for part in range(2):
-        @pl.when(has_left)
-        def _():
-            rightward[part].wait_recv()
-            gext[part, :, :ps] += xbuf[part]
-
-        c = remote(gext.at[part, ts:, :ts], ybuf.at[part], down_sem + part, me + TILE_COLS, z)
-        downward.append(c)
-
-        @pl.when(has_down)
-        def _():
-            c.start()
-
+    while len(todo) > 1:
+        serve()
+    margin(0)
     for s in streams:
         s.zg_wait()
         s.ag_start()
+    serve()
     for step in range(len(bits)):
         for s in streams:
             s.ag_wait()
@@ -478,6 +491,8 @@
                 s.ag_start()
             else:
                 s.pair_start()
+        if step == 0:
+            margin(1)
 
     for part in range(2):
         og_ref[part] = gext[part, :ts, :ts]
@@ -499,13 +514,14 @@
     for s in streams:
         s.copy.wait()
 
-    for stage in range(n_batch - 1):
-        for way in (1, -1):
-            sends, c = passing(way, stage)
-
-            @pl.when(sends)
-            def _():
-                c.wait_send()
+    for part in range(2):
+        for stage in range(hops):
+            for way in (1, -1):
+                sends, c = passing(way, stage, part)
+
+                @pl.when(sends)
+                def _():
+                    c.wait_send()
 
     def sent(i, carry):
         pair_copy(i).wait_send()
@@ -520,7 +536,7 @@
 
 def n_sems(n_tile, n_batch, mh, n_streams):
     n_bits = n_tile.bit_length() - 2
-    return 4 + mh + n_streams * (2 * n_bits + 2 * n_batch + 1) + 3 * n_batch + 4
+    return 4 + mh + n_streams * (2 * n_bits + 2 * n_batch + 1) + 5 * n_batch + 4
 
 
 def shards(n_tile, n_batch, object_tiles, probe, offsets, amplitude):

time: 153 us -> 139 us (0.908)
  Pallas kernels: 145 us -> 131 us
    pallas_call x1, Pallas kernels: 145 us -> 131 us  [shards(): pl.pallas_call(functools.partial(kernel, n_tile, n_batch), out_shape=(jax...]
where the time goes in v3:
time: 139 us
  Pallas kernels  131 us (94%)
  other arithmetic  4.66 us (3%)
  local copies, waits for them, and re-layouts  2.34 us (2%)
    pallas_call x1, Pallas kernels, shards(): pl.pallas_call(functools.partial(kernel, n_tile, n_batch), out_shape=(jax...  131 us
    mul x1, other arithmetic, shards(): pg.reshape(modes, 2, ps, ps) * (1.0 / math.sqrt(positions))  4.66 us

profile of v3, /device:TPU:0, one launch (start us, length us, event | category | flops | bytes accessed | tf_op | source)
XLA Modules:
  0.0 138.6 jit_solution(11356268603232968224)
XLA Ops:
  0.6 0.7 pad.4
  1.3 0.7 broadcast_in_dim.4.off_ref
  2.0 130.9 %ptycho.1 = (f32[2,384,384]{2,1,0:T(8,128)}, f32[4096,256]{1,0:T(8,128)}) custom-call(f32[2,384,384]{2,1,0:T(8,128)} %bitcast.7, s32[8,128]{1,0:T(8,128)} %broadcast_in_dim.4.off_ref, f32[256,256]{1,0:T(8,128)} %bitcast.8, bf16[8,2,256,256]{3,2,1,0:T(8,128)(2,1)} %probe_ref.1, bf16[4,768,256]{2,1,0:T(8,128)(2,1)} %constant.8.clone.right_ref, ...), custom_call_target="tpu_custom_call" | custom-call | flops 12999999488 | bytes 20000000 | tf_op jit(solution)/shard_map/ptycho/pallas_call | solution.py:554
  132.9 0.0 copy-start
  132.9 4.7 %broadcast_multiply_fusion = f32[4096,256]{1,0:T(8,128)} fusion(f32[4096,256]{1,0:T(8,128)} %get-tuple-element.5), kind=kLoop, calls=%fused_computation | loop fusion | flops 1048576 | bytes 8388608 | tf_op jit(solution)/shard_map/mul | solution.py:585
  137.5 0.0 copy-done
  137.6 1.0 copy.9
Async XLA Ops:
  132.9 4.7 %copy-start = (f32[2,384,384]{2,1,0:T(8,128)S(1)}, f32[2,384,384]{2,1,0:T(8,128)}, u32[]{:S(2)}) copy-start(f32[2,384,384]{2,1,0:T(8,128)} %get-tuple-element.4) | copy-start | bytes 3538948

commit v4 on v3

--- a/solution.py
+++ b/solution.py
@@ -73,7 +73,7 @@
 
 
 def kernel(n_tile, n_batch, tile_ref, off_ref, amp_ref, probe_ref, right_ref, left_ref,
-           og_ref, pg_ref, ext, patch, far, fac, ot, gext, acc, sendbuf, pairbuf, rsbuf, zbuf,
+           og_ref, pg_ref, ext, patch, far, fac, ot, gext, acc, sendbuf, pairbuf, rsbuf, zbuf, zfbuf,
            objbuf, offbuf, xbuf, ybuf, send_sem, recv_sem):
     me = lax.axis_index("tile")
     z = lax.axis_index("batch")
@@ -128,12 +128,15 @@
     for c in offs_out:
         c.start()
 
-    up = [
-        remote(tile_ref.at[:, :ps, :ps], ext.at[:, ts:, :ps], sems(), me - TILE_COLS, z),
-        remote(tile_ref.at[:, :ps, ps:], ext.at[:, ts:, ps:ts], sems(), me - TILE_COLS, z),
-    ]
+    own = lax.rem(z, 2)
+    twin = z + 1 - 2 * own
+    pieces = (slice(0, ps), slice(ps, ts))
+    up = [remote(tile_ref.at[own, :ps, c], ext.at[own, ts:, c], sems(), me - TILE_COLS, z)
+          for c in pieces]
+    share = [remote(ext.at[own, ts:, c], ext.at[own, ts:, c], sems(), me, twin) for c in pieces]
     leftward = remote(tile_ref.at[:, :, :ps], ext.at[:, :ts, ts:], sems(), me - 1, z)
-    corner = remote(ext.at[:, ts:, :ps], ext.at[:, ts:, ts:], sems(), me - 1, z)
+    corner = [remote(ext.at[part, ts:, :ps], ext.at[part, ts:, ts:], sems(), me - 1, z)
+              for part in (own, 1 - own)]
 
     @pl.when(has_up)
     def _():
@@ -167,14 +170,25 @@
     @pl.when(has_down)
     def _():
         up[0].wait_recv()
+        share[0].start()
 
     @pl.when(jnp.logical_and(has_down, has_left))
     def _():
-        corner.start()
+        corner[0].start()
 
     @pl.when(has_down)
     def _():
         up[1].wait_recv()
+        share[1].start()
+        share[0].wait_recv()
+
+    @pl.when(jnp.logical_and(has_down, has_left))
+    def _():
+        corner[1].start()
+
+    @pl.when(has_down)
+    def _():
+        share[1].wait_recv()
 
     @pl.when(has_right)
     def _():
@@ -182,7 +196,8 @@
 
     @pl.when(jnp.logical_and(has_down, has_right))
     def _():
-        corner.wait_recv()
+        corner[0].wait_recv()
+        corner[1].wait_recv()
 
     r_at = off_ref[0:1, 0:1]
     c_at = off_ref[1:2, 0:1]
@@ -205,7 +220,13 @@
 
     @pl.when(jnp.logical_and(has_down, has_left))
     def _():
-        corner.wait_send()
+        corner[0].wait_send()
+        corner[1].wait_send()
+
+    @pl.when(has_down)
+    def _():
+        share[0].wait_send()
+        share[1].wait_send()
 
     def forward(k, intensity):
         i0, i1 = intensity
@@ -275,8 +296,8 @@
     base_out = core * (mh * mode_rows)
 
     class Stream:
-        def __init__(self, index, order):
-            self.index, self.order = index, order
+        def __init__(self, index, order, z_first=False):
+            self.index, self.order, self.z_first = index, order, z_first
             self.first = index * length
             self.start, self.size, self.step = self.first, length, 0
             self.slot = 0
@@ -300,7 +321,7 @@
                 acc.at[self.rows(self.start + (1 - mine) * half, half)],
                 rsbuf.at[self.index, pl.ds(self.slot, half)],
                 self.sem_rs + self.step, self.partner, z)
-            if self.step:
+            if self.step or self.z_first:
                 self.copy.start()
             self.start = self.start + mine * half
             self.size = half
@@ -311,6 +332,39 @@
             acc[at] += rsbuf[self.index, self.slot:self.slot + self.size]
             self.slot += self.size
             self.step += 1
+
+        def zf_start(self):
+            q = length // n_batch
+            self.copies = []
+            for d in range(1, n_batch):
+                dest = lax.rem(z + d, n_batch)
+                c = remote(acc.at[self.rows(self.first + dest * q, q)], zfbuf.at[d],
+                           self.sem_z + d, me, dest)
+                c.start()
+                self.copies.append(c)
+
+        def zf_wait(self):
+            for c in self.copies:
+                c.wait()
+            self.size = length // n_batch
+            self.start = self.first + z * self.size
+            at = self.rows(self.start, self.size)
+            total = acc[at]
+            for d in range(1, n_batch):
+                total = total + zfbuf[d]
+            acc[at] = total
+
+        def settle(self):
+            pg_ref[self.rows(base_out + self.start, self.size)] = acc[self.rows(self.start, self.size)]
+
+        def zl_start(self):
+            q = length // n_batch
+            at = self.rows(base_out + self.first + z * q, q)
+            self.copies = []
+            for d in range(1, n_batch):
+                c = remote(pg_ref.at[at], pg_ref.at[at], self.sem_zg + d, me, lax.rem(z + d, n_batch))
+                c.start()
+                self.copies.append(c)
 
         def z_start(self):
             q = self.size // n_batch
@@ -369,8 +423,12 @@
                stream_base + i * stream_sems, me + bit * (1 - 2 * mine), z).start()
         return carry
 
-    lax.fori_loop(0, n_streams, summed, 0)
-    streams = [Stream(i, bits if i % 2 == 0 else bits[::-1]) for i in range(n_streams)]
+    for j in range(per_stream):
+        both(j)
+    around_z = Stream(0, bits, True)
+    around_z.zf_start()
+    lax.fori_loop(1, n_streams, summed, 0)
+    streams = [Stream(i, bits if i % 2 == 0 else bits[::-1]) for i in range(1, n_streams)]
     for s in streams:
         s.rs_start()
 
@@ -466,6 +524,11 @@
 
     for step in range(len(bits)):
         serve()
+        if step == 0:
+            around_z.zf_wait()
+        else:
+            around_z.rs_wait()
+        around_z.rs_start()
         for s in streams:
             s.rs_wait()
             if step + 1 < len(bits):
@@ -474,16 +537,24 @@
                 s.z_start()
     while len(todo) > hops:
         serve()
+    around_z.rs_wait()
+    around_z.settle()
+    around_z.ag_start()
     serve()
     for s in streams:
         s.z_wait()
     while len(todo) > 1:
         serve()
+    for step in range(len(bits) - 1):
+        around_z.ag_wait()
+        around_z.ag_start()
     margin(0)
     for s in streams:
         s.zg_wait()
         s.ag_start()
     serve()
+    around_z.ag_wait()
+    around_z.zl_start()
     for step in range(len(bits)):
         for s in streams:
             s.ag_wait()
@@ -493,6 +564,8 @@
                 s.pair_start()
         if step == 0:
             margin(1)
+    around_z.zg_wait()
+    around_z.pair_start()
 
     for part in range(2):
         og_ref[part] = gext[part, :ts, :ts]
@@ -511,7 +584,7 @@
         def _():
             downward[part].wait_send()
 
-    for s in streams:
+    for s in [*streams, around_z]:
         s.copy.wait()
 
     for part in range(2):
@@ -536,7 +609,7 @@
 
 def n_sems(n_tile, n_batch, mh, n_streams):
     n_bits = n_tile.bit_length() - 2
-    return 4 + mh + n_streams * (2 * n_bits + 2 * n_batch + 1) + 5 * n_batch + 4
+    return 7 + mh + n_streams * (2 * n_bits + 2 * n_batch + 1) + 5 * n_batch + 4
 
 
 def shards(n_tile, n_batch, object_tiles, probe, offsets, amplitude):
@@ -569,6 +642,7 @@
             pltpu.VMEM((half, ps), F32),
             pltpu.VMEM((n_streams, length, ps), F32),
             pltpu.VMEM((n_streams, n_batch, q, ps), F32),
+            pltpu.VMEM((n_batch, length // n_batch, ps), F32),
             pltpu.VMEM((n_batch, 2, ps, ps), F32),
             pltpu.VMEM((n_batch, 8, 128), jnp.int32),
             pltpu.VMEM((2, te, ps), F32),

time: 139 us -> 132 us (0.950)
  Pallas kernels: 131 us -> 125 us
    pallas_call x1, Pallas kernels: 131 us -> 125 us  [shards(): pl.pallas_call(functools.partial(kernel, n_tile, n_batch), out_shape=(jax...]
where the time goes in v4:
time: 132 us
  Pallas kernels  125 us (95%)
  other arithmetic  4.66 us (4%)
  local copies, waits for them, and re-layouts  2.34 us (2%)
    pallas_call x1, Pallas kernels, shards(): pl.pallas_call(functools.partial(kernel, n_tile, n_batch), out_shape=(jax...  125 us
    mul x1, other arithmetic, shards(): pg.reshape(modes, 2, ps, ps) * (1.0 / math.sqrt(positions))  4.66 us

profile of v4, /device:TPU:0, one launch (start us, length us, event | category | flops | bytes accessed | tf_op | source)
XLA Modules:
  0.0 132.2 jit_solution(6354283833457740929)
XLA Ops:
  0.6 0.7 pad.4
  1.3 0.7 broadcast_in_dim.4.off_ref
  2.0 124.6 %ptycho.1 = (f32[2,384,384]{2,1,0:T(8,128)}, f32[4096,256]{1,0:T(8,128)}) custom-call(f32[2,384,384]{2,1,0:T(8,128)} %bitcast.7, s32[8,128]{1,0:T(8,128)} %broadcast_in_dim.4.off_ref, f32[256,256]{1,0:T(8,128)} %bitcast.8, bf16[8,2,256,256]{3,2,1,0:T(8,128)(2,1)} %probe_ref.1, bf16[4,768,256]{2,1,0:T(8,128)(2,1)} %constant.8.clone.right_ref, ...), custom_call_target="tpu_custom_call" | custom-call | flops 12999999488 | bytes 20000000 | tf_op jit(solution)/shard_map/ptycho/pallas_call | solution.py:627
  126.6 0.0 copy-start
  126.6 4.7 %broadcast_multiply_fusion = f32[4096,256]{1,0:T(8,128)} fusion(f32[4096,256]{1,0:T(8,128)} %get-tuple-element.5), kind=kLoop, calls=%fused_computation | loop fusion | flops 1048576 | bytes 8388608 | tf_op jit(solution)/shard_map/mul | solution.py:659
  131.2 0.0 copy-done
  131.2 1.0 copy.9
Async XLA Ops:
  126.6 4.7 %copy-start = (f32[2,384,384]{2,1,0:T(8,128)S(1)}, f32[2,384,384]{2,1,0:T(8,128)}, u32[]{:S(2)}) copy-start(f32[2,384,384]{2,1,0:T(8,128)} %get-tuple-element.4) | copy-start | bytes 3538948

commit v5 on v4

--- a/solution.py
+++ b/solution.py
@@ -72,9 +72,10 @@
     return jnp.where(hit, 1.0, 0.0).astype(F32).astype(BF16)
 
 
-def kernel(n_tile, n_batch, tile_ref, off_ref, amp_ref, probe_ref, right_ref, left_ref,
-           og_ref, pg_ref, ext, patch, far, fac, ot, gext, acc, sendbuf, pairbuf, rsbuf, zbuf, zfbuf,
-           objbuf, offbuf, xbuf, ybuf, send_sem, recv_sem):
+def kernel(n_tile, n_batch, tile_ref, offsets_ref, amp_hbm, probe_hbm, right_hbm, left_hbm,
+           og_hbm, pg_hbm, amp_ref, probe_ref, right_ref, left_ref, off_ref, og_ref, pg_ref, ext, patch, far, fac, ot, gext, acc, sendbuf, pairbuf, rsbuf, zbuf, zfbuf,
+           objbuf, offbuf, xbuf, ybuf, send_sem, recv_sem, load_sem,
+           out_sem):
     me = lax.axis_index("tile")
     z = lax.axis_index("batch")
     ts = tile_ref.shape[-1]
@@ -105,6 +106,13 @@
             src_ref=src, dst_ref=dst, send_sem=send_sem.at[sem], recv_sem=recv_sem.at[sem],
             device_id=(tile, batch), device_id_type=MESH)
 
+    loads = [pltpu.make_async_copy(src, dst, load_sem.at[i]) for i, (src, dst) in enumerate(
+        ((amp_hbm, amp_ref), (probe_hbm, probe_ref), (right_hbm, right_ref), (left_hbm, left_ref)))]
+    for c in loads:
+        c.start()
+    off_ref[...] = jnp.where(lax.broadcasted_iota(jnp.int32, off_ref.shape, 0) == 0,
+                             offsets_ref[0, 0, 0], offsets_ref[0, 0, 1])
+
     barrier = pltpu.get_barrier_semaphore()
 
     def greet(tile, batch):
@@ -161,6 +169,7 @@
     def _():
         ext[:, ts:, ts:] = jnp.zeros((2, ps, ps), F32)
 
+    loads[0].wait()
     rows = lax.broadcasted_iota(jnp.int32, (ps, ps), 0)
     cols = lax.broadcasted_iota(jnp.int32, (ps, ps), 1)
     by_row = onehot(cols == jnp.where(rows < h, 2 * rows, 2 * (rows - h) + 1))
@@ -227,6 +236,9 @@
     def _():
         share[0].wait_send()
         share[1].wait_send()
+
+    for c in loads[1:]:
+        c.wait()
 
     def forward(k, intensity):
         i0, i1 = intensity
@@ -540,10 +552,9 @@
     around_z.rs_wait()
     around_z.settle()
     around_z.ag_start()
-    serve()
     for s in streams:
         s.z_wait()
-    while len(todo) > 1:
+    while len(todo) > 2:
         serve()
     for step in range(len(bits) - 1):
         around_z.ag_wait()
@@ -552,7 +563,8 @@
     for s in streams:
         s.zg_wait()
         s.ag_start()
-    serve()
+    while todo:
+        serve()
     around_z.ag_wait()
     around_z.zl_start()
     for step in range(len(bits)):
@@ -567,6 +579,21 @@
     around_z.zg_wait()
     around_z.pair_start()
 
+    outs = []
+
+    def write_out(src, dst):
+        c = pltpu.make_async_copy(src, dst, out_sem.at[len(outs)])
+        c.start()
+        outs.append(c)
+
+    def write_stream(s):
+        s.copy.wait()
+        for side in range(2):
+            at = pl.ds(side * mh * mode_rows + s.first, length)
+            write_out(pg_ref.at[at], pg_hbm.at[at])
+
+    for s in streams:
+        write_stream(s)
     for part in range(2):
         og_ref[part] = gext[part, :ts, :ts]
 
@@ -575,6 +602,9 @@
             downward[part].wait_recv()
             og_ref[part, :ps, :] += ybuf[part]
 
+        write_out(og_ref.at[part], og_hbm.at[part])
+    write_stream(around_z)
+
     for part in range(2):
         @pl.when(has_right)
         def _():
@@ -584,9 +614,6 @@
         def _():
             downward[part].wait_send()
 
-    for s in [*streams, around_z]:
-        s.copy.wait()
-
     for part in range(2):
         for stage in range(hops):
             for way in (1, -1):
@@ -601,6 +628,8 @@
         return carry
 
     lax.fori_loop(0, mh, sent, 0)
+    for c in outs:
+        c.wait()
 
 
 def streams_of(n_tile, n_batch, mh, mode_rows):
@@ -617,20 +646,28 @@
     ts = object_tiles.shape[-1]
     te = ts + ps
     rights, lefts = dft_tables(ps)
-    held = jnp.broadcast_to(jnp.pad(offsets[0, 0], (0, 6))[:, None], (8, 128))
     n_streams = streams_of(n_tile, n_batch, modes // 2, 2 * ps)
     n = n_sems(n_tile, n_batch, modes // 2, n_streams)
     half = modes // 2 * 2 * ps
     length = half // n_streams
     q = length // (n_tile // 2) // n_batch
     vmem = pl.BlockSpec(memory_space=pltpu.VMEM)
+    smem = pl.BlockSpec(memory_space=pltpu.SMEM)
+    anywhere = pl.BlockSpec(memory_space=pl.ANY)
     og, pg = pl.pallas_call(
         functools.partial(kernel, n_tile, n_batch),
         out_shape=(jax.ShapeDtypeStruct((2, ts, ts), F32),
                    jax.ShapeDtypeStruct((modes * 2 * ps, ps), F32)),
-        in_specs=[vmem] * 6,
-        out_specs=(vmem, vmem),
+        in_specs=[vmem, smem, anywhere, anywhere, anywhere, anywhere],
+        out_specs=(anywhere, anywhere),
         scratch_shapes=[
+            pltpu.VMEM((ps, ps), F32),
+            pltpu.VMEM(probe.shape, probe.dtype),
+            pltpu.VMEM(rights.shape, BF16),
+            pltpu.VMEM(lefts.shape, BF16),
+            pltpu.VMEM((8, 128), jnp.int32),
+            pltpu.VMEM((2, ts, ts), F32),
+            pltpu.VMEM((modes * 2 * ps, ps), F32),
             pltpu.VMEM((2, te, te), F32),
             pltpu.VMEM((2, ps, ps), F32),
             pltpu.VMEM((modes, 2, ps, ps), F32),
@@ -649,12 +686,14 @@
             pltpu.VMEM((2, ps, ts), F32),
             pltpu.SemaphoreType.DMA((n,)),
             pltpu.SemaphoreType.DMA((n,)),
+            pltpu.SemaphoreType.DMA((4,)),
+            pltpu.SemaphoreType.DMA((2 * n_streams + 2,)),
         ],
         compiler_params=pltpu.CompilerParams(
             collective_id=0, has_side_effects=True, vmem_limit_bytes=56 * 1024 * 1024),
         cost_estimate=pl.CostEstimate(flops=13_000_000_000, bytes_accessed=20_000_000, transcendentals=0),
         name="ptycho",
-    )(object_tiles[0], held, amplitude[0, 0], probe, rights, lefts)
+    )(object_tiles[0], offsets, amplitude[0, 0], probe, rights, lefts)
     positions = n_tile * n_batch * offsets.shape[1]
     return og[None], pg.reshape(modes, 2, ps, ps) * (1.0 / math.sqrt(positions))
 

time: 132 us -> 127 us (0.962)
  Pallas kernels: 125 us -> 120 us
    pallas_call x1, Pallas kernels: 125 us -> 120 us  [shards(): pl.pallas_call(functools.partial(kernel, n_tile, n_batch), out_shape=(jax...]
where the time goes in v5:
time: 127 us; the launch traced here: 126 us
  Pallas kernels  120 us (94%)
  other arithmetic  4.66 us (4%)
    pallas_call x1, Pallas kernels, shards(): pl.pallas_call(functools.partial(kernel, n_tile, n_batch), out_shape=(jax...  120 us
    mul x1, other arithmetic, shards(): pg.reshape(modes, 2, ps, ps) * (1.0 / math.sqrt(positions))  4.66 us

profile of v5, /device:TPU:0, one launch (start us, length us, event | category | flops | bytes accessed | tf_op | source)
XLA Modules:
  0.0 126.4 jit_solution(4219187889534470059)
XLA Ops:
  0.6 120.1 %ptycho.1 = (f32[2,384,384]{2,1,0:T(8,128)}, f32[4096,256]{1,0:T(8,128)}) custom-call(f32[2,384,384]{2,1,0:T(8,128)} %bitcast.6, s32[1,1,2]{2,1,0:T(1,128)} %offsets_ref.1, f32[256,256]{1,0:T(8,128)} %bitcast.7, bf16[8,2,256,256]{3,2,1,0:T(8,128)(2,1)} %probe_hbm.1, bf16[4,768,256]{2,1,0:T(8,128)(2,1)} %constant.6.clone.right_hbm, ...), custom_call_target="tpu_custom_call" | custom-call | flops 12999999488 | bytes 20000000 | tf_op jit(solution)/shard_map/ptycho/pallas_call | solution.py:657
  120.8 0.0 copy-start
  120.8 4.7 %broadcast_multiply_fusion = f32[4096,256]{1,0:T(8,128)} fusion(f32[4096,256]{1,0:T(8,128)} %get-tuple-element.5), kind=kLoop, calls=%fused_computation | loop fusion | flops 1048576 | bytes 8388608 | tf_op jit(solution)/shard_map/mul | solution.py:698
  125.4 0.0 copy-done
  125.4 1.0 copy.9
Async XLA Ops:
  120.8 4.7 %copy-start = (f32[2,384,384]{2,1,0:T(8,128)S(1)}, f32[2,384,384]{2,1,0:T(8,128)}, u32[]{:S(2)}) copy-start(f32[2,384,384]{2,1,0:T(8,128)} %get-tuple-element.4) | copy-start | bytes 3538948

commit v6 on v5

--- a/solution.py
+++ b/solution.py
@@ -639,6 +639,11 @@
 def n_sems(n_tile, n_batch, mh, n_streams):
     n_bits = n_tile.bit_length() - 2
     return 7 + mh + n_streams * (2 * n_bits + 2 * n_batch + 1) + 5 * n_batch + 4
+
+
+def finish(scale, og_ref, pg_ref, og_out, pg_out):
+    og_out[...] = og_ref[...]
+    pg_out[...] = pg_ref[...] * scale
 
 
 def shards(n_tile, n_batch, object_tiles, probe, offsets, amplitude):
@@ -695,7 +700,17 @@
         name="ptycho",
     )(object_tiles[0], offsets, amplitude[0, 0], probe, rights, lefts)
     positions = n_tile * n_batch * offsets.shape[1]
-    return og[None], pg.reshape(modes, 2, ps, ps) * (1.0 / math.sqrt(positions))
+    probe_spec = pl.BlockSpec((modes * 2 * ps // 8, ps), lambda i: (i, 0))
+    object_spec = pl.BlockSpec((2, ts // 8, ts), lambda i: (0, i, 0))
+    og, pg = pl.pallas_call(
+        functools.partial(finish, 1.0 / math.sqrt(positions)),
+        out_shape=(jax.ShapeDtypeStruct(og.shape, F32), jax.ShapeDtypeStruct(pg.shape, F32)),
+        grid=(8,),
+        in_specs=[object_spec, probe_spec],
+        out_specs=(object_spec, probe_spec),
+        name="finish",
+    )(og, pg)
+    return og[None], pg.reshape(modes, 2, ps, ps)
 
 
 def solution(mesh):

time: 127 us -> 129 us (1.016)
  Pallas kernels: 120 us -> 128 us
  other arithmetic: 4.66 us -> 0 us
    pallas_call x0 -> x1, Pallas kernels: none -> 7.43 us  [shards(): pl.pallas_call(functools.partial(finish, 1.0 / math.sqrt(positions)), out...]
    mul x1 -> x0, other arithmetic: 4.66 us -> none  [shards(): pg.reshape(modes, 2, ps, ps) * (1.0 / math.sqrt(positions))]
where the time goes in v6:
time: 129 us; the launch traced here: 128 us
  Pallas kernels  128 us (99%)
    pallas_call x1, Pallas kernels, shards(): pl.pallas_call(functools.partial(kernel, n_tile, n_batch), out_shape=(jax...  120 us
    pallas_call x1, Pallas kernels, shards(): pl.pallas_call(functools.partial(finish, 1.0 / math.sqrt(positions)), out...  7.43 us

profile of v6, /device:TPU:0, one launch (start us, length us, event | category | flops | bytes accessed | tf_op | source)
XLA Modules:
  0.0 128.4 jit_solution(3849782807857736259)
XLA Ops:
  0.6 120.3 %ptycho.1 = (f32[2,384,384]{2,1,0:T(8,128)}, f32[4096,256]{1,0:T(8,128)}) custom-call(f32[2,384,384]{2,1,0:T(8,128)} %bitcast.5, s32[1,1,2]{2,1,0:T(1,128)} %offsets_ref.1, f32[256,256]{1,0:T(8,128)} %bitcast.7, bf16[8,2,256,256]{3,2,1,0:T(8,128)(2,1)} %probe_hbm.1, bf16[4,768,256]{2,1,0:T(8,128)(2,1)} %constant.4.clone.right_hbm, ...), custom_call_target="tpu_custom_call" | custom-call | flops 12999999488 | bytes 20000000 | tf_op jit(solution)/shard_map/ptycho/pallas_call | solution.py:662
  121.0 7.4 %finish.1 = (f32[2,384,384]{2,1,0:T(8,128)}, f32[4096,256]{1,0:T(8,128)}) custom-call(f32[2,384,384]{2,1,0:T(8,128)} %get-tuple-element.6.og_ref, f32[4096,256]{1,0:T(8,128)} %get-tuple-element.7.pg_ref), custom_call_target="tpu_custom_call" | custom-call | tf_op jit(solution)/shard_map/finish/pallas_call | solution.py:705
